TPU v7x, 256 devices: a whole 4x4x8 slice. The times are simulated.
256 devices in a mesh: rows: 64 (over z, x, core), cols: 4 (over y).
Axes of the slice: x: 4, y: 4, z: 8, core: 2. Of those that a mesh axis runs over, the one named last changes fastest.
Arguments:
- matrix_t: float32 [256, 524288], P('cols', 'rows'), may hold values from -6 to 6
- signs: int32 [524288], P('rows'), may hold values from -1 to 1, as said below
- sample_ids: int32 [16384], P('rows'), may hold values from 0 to 524287, as said below
Outputs:
- sketch: float32 [256, 16384], P('cols', 'rows')
- gram: float32 [256, 256], P('cols')
Inputs may be any that keep to these rules, and one draw needn't show every extreme that they name: `sample_ids`: sketch rows come in 64 owner blocks of 256; inside owner block o, positions s * 4 to (s + 1) * 4 - 1 name rows of row block s (rows s * 8192 to (s + 1) * 8192 - 1); no row is named twice. The ids may cross between devices in any lossless encoding, several packed into one 32-bit word. `signs`: each entry is -1 or 1.
All inputs are finite; a program needn't handle non-finite values.
Results may differ from a plain program's by a relative error of at most 0.00013.
Values sent between devices are 32-bit elements; how exact they have to be, the bound alone decides.
A program may use at most 64 MiB of HBM per device.

v0:
```python
import jax
import jax.numpy as jnp
from jax import lax
from jax.sharding import PartitionSpec as P


def partner_2(shard, axis, distance):
    return lax.ppermute(shard, axis, [(i, i ^ 1 << distance) for i in range(lax.axis_size(axis))])


def sylvester(order):
    index = jnp.arange(order, dtype=jnp.int32)
    parity = jnp.zeros((order, order), jnp.int32)
    width = max(order.bit_length() - 1, 0)
    for bit in range(width):
        parity = parity + (index[:, None] >> bit & 1) * (index[None, :] >> bit & 1)
    return (1 - 2 * (parity % 2)).astype(jnp.float32)


def on_device(matrix_t, signs, sample_ids):
    high = lax.Precision.HIGHEST
    local_cols, local_rows = matrix_t.shape
    blocks_count = lax.axis_size("rows")
    total = local_rows * blocks_count
    me_row = lax.axis_index("rows")
    inner = local_rows // 128
    signed = matrix_t * signs.astype(jnp.float32)[None, :]
    shaped = signed.reshape(local_cols, 128, inner)
    shaped = jnp.einsum("ab,cbq->caq", sylvester(128), shaped, precision=high)
    shaped = jnp.einsum("pq,caq->cap", sylvester(inner), shaped, precision=high)
    mixed = shaped.reshape(local_cols, local_rows)
    pair = sample_ids.shape[0] // blocks_count
    for bit in range(blocks_count.bit_length() - 1):
        partner = partner_2(mixed, "rows", bit)
        upper = me_row >> bit & 1
        mixed = jnp.where(upper == 1, partner - mixed, mixed + partner)
    transformed = mixed * (1.0 / total**0.5)
    every_id = lax.all_gather(sample_ids, "rows", axis=0, tiled=True)
    grid = every_id.reshape(blocks_count, blocks_count, pair)
    wanted = lax.dynamic_index_in_dim(grid, me_row, 1, keepdims=False)
    local_index = (wanted - me_row * local_rows).reshape(-1)
    outgoing = jnp.take(transformed, local_index, axis=1).reshape(local_cols, blocks_count, pair)
    arrived = lax.all_to_all(outgoing, "rows", split_axis=1, concat_axis=1, tiled=True)
    sketch = arrived.reshape(local_cols, blocks_count * pair)
    full_rows = lax.all_gather(sketch, "cols", axis=0, tiled=True)
    partial_value = jnp.dot(sketch, full_rows.T, precision=high, preferred_element_type=jnp.float32)
    summed = lax.psum(partial_value, "rows")
    gram = summed / (sample_ids.shape[0] * blocks_count)
    return (sketch, gram)


def solution(mesh):
    placed = (P("cols", "rows"), P("rows"), P("rows"))
    return jax.shard_map(
        on_device,
        mesh=mesh,
        in_specs=placed,
        out_specs=(P("cols", "rows"), P("cols", None)),
        check_vma=False,
    )
```

profile of v0, /device:TPU:1, one launch (start us, length us, event | category | flops | bytes accessed | tf_op | source)
XLA Modules:
  0.0 681.6 jit_solution(9767158852562128828)
XLA Ops:
  7.2 0.0 all-reduce.2.cloned.1.call-start
  7.3 0.8 convert_element_type.9
  8.0 1.7 broadcast_multiply_fusion
  9.8 3.0 reshape.238
  12.8 8.7 %fusion.7 = f32[64,64,128]{2,1,0:T(8,128)S(1)} fusion(f32[64,128,64]{2,1,0:T(8,128)} %reshape.238, s32[128]{0:T(128)S(1)} %get-tuple-element.10, s32[128]{0:T(128)S(1)} %get-tuple-element.11, s32[128]{0:T(128)S(1)} %get-tuple-element.12, s32[128]{0:T(128)S(1)} %get-tuple-element.13, s32[128]{0:T(128)S(1)} %get-tuple-element.14, ...), kind=kOutput, calls=%fused_computation.18 | convolution fusion | flops 805748736 | bytes 4197888 | tf_op jit(solution)/shard_map/ab,cbq->caq/dot_general | solution.py:29
  21.6 8.4 %fusion = f32[64,128,64]{2,1,0:T(8,128)} fusion(f32[64,64,128]{2,1,0:T(8,128)S(1)} %fusion.7, s32[64]{0:T(128)S(1)} %get-tuple-element.16, s32[64]{0:T(128)S(1)} %get-tuple-element.17, s32[64]{0:T(128)S(1)} %get-tuple-element.18, s32[64]{0:T(128)S(1)} %get-tuple-element.19, s32[64]{0:T(128)S(1)} %get-tuple-element.20, s32[64]{0:T(128)S(1)} %get-tuple-element.21), kind=kOutput, calls=%fused_computation.7 | convolution fusion | flops 402755584 | bytes 4195840 | tf_op jit(solution)/shard_map/pq,caq->cap/dot_general | solution.py:30
  30.0 3.5 reshape.239
  33.5 3.3 collective-permute-start
  36.8 2.7 copy.27
  39.6 1.2 collective-permute-done
  40.7 3.8 copy.26
  44.5 5.9 add_select_fusion.4
  50.4 3.8 copy.30
  54.2 0.0 collective-permute-start.1
  54.2 47.1 %collective-permute-done.1 = f32[64,8192]{1,0:T(8,128)S(1)} collective-permute-done((f32[64,8192]{1,0:T(8,128)}, f32[64,8192]{1,0:T(8,128)S(1)}, u32[]{:S(2)}, u32[]{:S(2)}) %collective-permute-start.1) | collective-permute-done | bytes 2097184 | tf_op jit(solution)/shard_map/ppermute | solution.py:8
  101.3 2.7 copy.31
  104.0 5.9 add_select_fusion.3
  109.8 3.8 copy.33
  113.6 1.0 collective-permute-start.2
  114.7 46.6 %collective-permute-done.2 = f32[64,8192]{1,0:T(8,128)S(1)} collective-permute-done((f32[64,8192]{1,0:T(8,128)}, f32[64,8192]{1,0:T(8,128)S(1)}, u32[]{:S(2)}, u32[]{:S(2)}) %collective-permute-start.2) | collective-permute-done | bytes 2097184 | tf_op jit(solution)/shard_map/ppermute | solution.py:8
  161.3 2.7 copy.34
  164.0 5.9 add_select_fusion.2
  169.9 3.8 copy.36
  173.7 0.0 collective-permute-start.3
  173.7 45.2 %collective-permute-done.3 = f32[64,8192]{1,0:T(8,128)S(1)} collective-permute-done((f32[64,8192]{1,0:T(8,128)}, f32[64,8192]{1,0:T(8,128)S(1)}, u32[]{:S(2)}, u32[]{:S(2)}) %collective-permute-start.3) | collective-permute-done | bytes 2097184 | tf_op jit(solution)/shard_map/ppermute | solution.py:8
  218.9 2.7 copy.37
  221.6 5.9 add_select_fusion.1
  227.5 3.8 copy.39
  231.3 1.6 collective-permute-start.4
  232.9 91.8 %collective-permute-done.4 = f32[64,8192]{1,0:T(8,128)S(1)} collective-permute-done((f32[64,8192]{1,0:T(8,128)}, f32[64,8192]{1,0:T(8,128)S(1)}, u32[]{:S(2)}, u32[]{:S(2)}) %collective-permute-start.4) | collective-permute-done | bytes 2097184 | tf_op jit(solution)/shard_map/ppermute | solution.py:8
  324.6 2.7 copy.40
  327.3 5.9 add_select_fusion
  333.2 0.0 copy-start.1
  333.2 3.8 copy.42
  337.0 4.9 collective-permute-start.5
  341.9 0.0 copy-done.1
  341.9 125.3 %all-gather = s32[64,1,256]{2,1,0:T(1,128)S(1)} all-gather(s32[1,1,256]{2,1,0:T(1,128)S(1)} %bitcast.33), channel_id=1, replica_groups=mesh['rows'=64,'cols'=4] {'rows'}, dimensions={0}, use_global_device_ids=true | all-gather | bytes 66560 | tf_op jit(solution)/shard_map/all_gather | solution.py:38
  467.2 0.1 copy.22
  467.3 0.1 copy.45
  467.4 0.1 sub.66
  467.5 0.1 copy.23
  467.7 0.0 collective-permute-done.5
  467.7 2.7 copy.43
  470.4 6.0 select_multiply_fusion
  476.4 2.9 gather_fusion
  479.3 0.1 fusion.59
  479.4 0.1 reshape.254
  479.6 16.2 %all_to_all.5 = f32[64,1,256]{2,1,0:T(1,128)S(1)} all-to-all(f32[64,1,256]{2,1,0:T(1,128)S(1)} %reshape.254), channel_id=1, replica_groups=mesh['rows'=64,'cols'=4] {'rows'}, dimensions={0} | all-to-all | bytes 131072 | tf_op jit(solution)/shard_map/all_to_all | solution.py:43
  495.8 0.5 broadcast.357
  496.3 0.8 reduce
  497.1 0.1 reshape.255
  497.2 0.1 copy.47
  497.3 0.0 copy-start
  497.3 10.3 %all_gather.7 = f32[256,256]{1,0:T(8,128)S(1)} all-gather(f32[64,256]{1,0:T(8,128)S(1)} %copy.47), channel_id=1, replica_groups=mesh['rows'=64,'cols'=4] {'cols'}, dimensions={0}, use_global_device_ids=true | all-gather | bytes 327680 | tf_op jit(solution)/shard_map/all_gather | solution.py:45
  507.6 1.0 fusion.60
  508.7 0.0 all-reduce.2.cloned.1.call-update
  508.7 164.6 %all-reduce.2.cloned.1.call-done = f32[64,256]{1,0:T(8,128)} async-done(((f32[64,256]{1,0:T(8,128)}), f32[64,256]{1,0:T(8,128)}) %all-reduce.2.cloned.1.call-update) | async-done | bytes 65552 | tf_op jit(solution)/shard_map/psum | solution.py:47
  673.2 1.5 broadcast_multiply_fusion.1
  674.7 0.0 copy-done
  (10 shorter events, 0.1 us)
Async XLA Ops:
  7.2 666.1 %all-reduce.2.cloned.1.call-start = ((), (), s32[]{:S(2)}) async-start(), calls=%async_computation.1 | async-start | bytes 131072 | tf_op jit(solution)/shard_map/psum | solution.py:47
  33.5 7.2 %collective-permute-start = (f32[64,8192]{1,0:T(8,128)S(1)}, f32[64,8192]{1,0:T(8,128)}, u32[]{:S(2)}, u32[]{:S(2)}) collective-permute-start(f32[64,8192]{1,0:T(8,128)S(1)} %reshape.239), channel_id=1, source_target_pairs={{0,4},{4,0},{8,12},{12,8},{16,20},{20,16},{24,28},{28,24},{32,36},... | collective-permute-start | bytes 6291464 | tf_op jit(solution)/shard_map/ppermute | solution.py:8
  54.2 47.1 %collective-permute-start.1 = (f32[64,8192]{1,0:T(8,128)}, f32[64,8192]{1,0:T(8,128)S(1)}, u32[]{:S(2)}, u32[]{:S(2)}) collective-permute-start(f32[64,8192]{1,0:T(8,128)} %copy.30), channel_id=1, source_target_pairs={{0,8},{4,12},{8,0},{12,4},{16,24},{20,28},{24,16},{28,20},{32,40},... | collective-permute-start | bytes 6291464 | tf_op jit(solution)/shard_map/ppermute | solution.py:8
  113.6 47.6 %collective-permute-start.2 = (f32[64,8192]{1,0:T(8,128)}, f32[64,8192]{1,0:T(8,128)S(1)}, u32[]{:S(2)}, u32[]{:S(2)}) collective-permute-start(f32[64,8192]{1,0:T(8,128)} %copy.33), channel_id=1, source_target_pairs={{0,16},{4,20},{8,24},{12,28},{16,0},{20,4},{24,8},{28,12},{32,48},... | collective-permute-start | bytes 6291464 | tf_op jit(solution)/shard_map/ppermute | solution.py:8
  173.7 45.2 %collective-permute-start.3 = (f32[64,8192]{1,0:T(8,128)}, f32[64,8192]{1,0:T(8,128)S(1)}, u32[]{:S(2)}, u32[]{:S(2)}) collective-permute-start(f32[64,8192]{1,0:T(8,128)} %copy.36), channel_id=1, source_target_pairs={{0,32},{4,36},{8,40},{12,44},{16,48},{20,52},{24,56},{28,60},{32,0... | collective-permute-start | bytes 6291464 | tf_op jit(solution)/shard_map/ppermute | solution.py:8
  231.3 93.4 %collective-permute-start.4 = (f32[64,8192]{1,0:T(8,128)}, f32[64,8192]{1,0:T(8,128)S(1)}, u32[]{:S(2)}, u32[]{:S(2)}) collective-permute-start(f32[64,8192]{1,0:T(8,128)} %copy.39), channel_id=1, source_target_pairs={{0,64},{4,68},{8,72},{12,76},{16,80},{20,84},{24,88},{28,92},{32,9... | collective-permute-start | bytes 6291464 | tf_op jit(solution)/shard_map/ppermute | solution.py:8
  333.2 8.7 %copy-start.1 = (s32[256]{0:T(256)S(1)}, s32[256]{0:T(256)}, u32[]{:S(2)}) copy-start(s32[256]{0:T(256)} %param.5) | copy-start | bytes 3076
  337.0 130.6 %collective-permute-start.5 = (f32[64,8192]{1,0:T(8,128)}, f32[64,8192]{1,0:T(8,128)S(1)}, u32[]{:S(2)}, u32[]{:S(2)}) collective-permute-start(f32[64,8192]{1,0:T(8,128)} %copy.42), channel_id=1, source_target_pairs={{0,128},{4,132},{8,136},{12,140},{16,144},{20,148},{24,152},{28,15... | collective-permute-start | bytes 6291464 | tf_op jit(solution)/shard_map/ppermute | solution.py:8
  497.3 177.4 %copy-start = (f32[64,256]{1,0:T(8,128)}, f32[64,256]{1,0:T(8,128)S(1)}, u32[]{:S(2)}) copy-start(f32[64,256]{1,0:T(8,128)S(1)} %copy.47) | copy-start | bytes 196612
Sparse Core Ops, SparseCore 0:
  508.8 164.3 all-reduce.1
where the time goes:
time: 682 us
  waiting for transfers between devices  396 us (58%)
  blocking collectives  152 us (22%)
  local copies, waits for them, and re-layouts  49.9 us (7%)
  other arithmetic  40.3 us (6%)
  matrix products  18.2 us (3%)
  between operations  14.2 us (2%)
  starting transfers between devices  10.9 us (2%)
    ppermute x6, waiting for transfers between devices, partner_2(): lax.ppermute(shard, axis, [(i, i ^ 1 << distance) for i in range(lax.axis...  232 us
    psum x1, waiting for transfers between devices, on_device(): summed = lax.psum(partial_value, 'rows')  165 us
    all_gather x1, blocking collectives, on_device(): every_id = lax.all_gather(sample_ids, 'rows', axis=0, tiled=True)  125 us
    select_n x5, other arithmetic, on_device(): mixed = jnp.where(upper == 1, partner - mixed, mixed + partner)  29.3 us
    select_n x5, local copies, waits for them, and re-layouts, on_device(): mixed = jnp.where(upper == 1, partner - mixed, mixed + partner)  19.1 us
    ppermute x6, local copies, waits for them, and re-layouts, partner_2(): lax.ppermute(shard, axis, [(i, i ^ 1 << distance) for i in range(lax.axis...  17.4 us
    all_to_all x1, blocking collectives, on_device(): lax.all_to_all(outgoing, 'rows', split_axis=1, concat_axis=1, tiled=True)  16.2 us
  transfers between devices with their start and end apart: 7, of which 6 were waited for; matrix products, arithmetic and copies ran while one was open for 0% of the time, Pallas kernels for 0%

commit v1 on v0

v1 whole, which is shorter than its diff:
```python
import jax
import jax.numpy as jnp
from jax import lax
from jax.experimental import pallas as pl
from jax.experimental.pallas import tpu as pltpu
from jax.sharding import PartitionSpec as P

MESH = pl.DeviceIdType.MESH
F32, BF16, I32 = jnp.float32, jnp.bfloat16, jnp.int32

NX, NZ, NY = 4, 8, 4
CHIPS = NX * NZ
COLS, ROWS = 64, 8192
KEEP = 4
LIST = CHIPS * KEEP
RA = 80
HA = RA // 2
RB = LIST - RA
HB = RB // 2
GA, GB = 4, 2
PA, PB = NZ // GA, NX // GB
UA, UB = 20, 24


def hadamard_rows(copies):
    shape = (128, 128 * copies)
    parity = lax.broadcasted_iota(I32, shape, 0) & lax.broadcasted_iota(I32, shape, 1) & 127
    for shift in (4, 2, 1):
        parity = parity ^ (parity >> shift)
    return (1 - 2 * (parity & 1)).astype(F32).astype(BF16)


def butterflies(parts):
    for stride in (1, 2, 4):
        done = list(parts)
        for i in range(8):
            if not i & stride:
                done[i] = parts[i] + parts[i | stride]
                done[i | stride] = parts[i] - parts[i | stride]
        parts = done
    return parts


def kernel(
    m_ref, s_ref, id_ref, sk_ref, g_ref,
    x_v, xp_v, sp_v, y_v, t_v, idp_v, ids_v, ids_s, sg_v,
    a1s, a1r, a2s, a2r, a_sum, azr,
    b1s, b1r, b2s, b2r, b_sum, bxr,
    f_v, fp_v, p_v, g1r, g2r, g3r,
    lx_sem, sm_sem, xs_sem, xr_sem, ps_sem, pr_sem, is_sem, ir_sem, rs_sem, rr_sem,
    gs_sem, gr_sem,
):
    me, y = lax.axis_index("rows"), lax.axis_index("cols")
    core, chip = me % 2, me // 2
    x, z = chip % NX, chip // NX
    corner = x * 2 + core

    def at(x_to, z_to, core_to):
        return {"rows": (lax.rem(z_to + NZ, NZ) * NX + lax.rem(x_to + NX, NX)) * 2 + core_to}

    partner = at(x, z, 1 - core)

    def remote(src, dst, send, recv, device):
        return pltpu.make_async_remote_copy(
            src_ref=src, dst_ref=dst, send_sem=send, recv_sem=recv, device_id=device, device_id_type=MESH
        )

    def own_copy(q):
        piece = pl.ds(pl.multiple_of(q * 1024, 1024), 1024)
        return pltpu.make_async_copy(m_ref.at[:, piece], x_v.at[q], lx_sem.at[q])

    for q in range(8):
        own_copy(q).start()

    barrier = pltpu.get_barrier_semaphore()

    def greet(device):
        pl.semaphore_signal(barrier, inc=1, device_id=device, device_id_type=MESH)

    greet(partner)

    def greet_chip(o, _):
        to = lax.rem(chip + o, CHIPS)
        greet({"rows": to * 2 + core})
        return 0

    lax.fori_loop(1, CHIPS, greet_chip, 0)
    for o in range(1, NX):
        greet(at(x + o, z, 1 - core))
    for o in range(1, NY):
        greet({"cols": lax.rem(y + o, NY)})
    pl.semaphore_wait(barrier, 1 + CHIPS - 1 + NX - 1 + NY - 1)

    ids_out = remote(id_ref.at[1 - core], idp_v, ps_sem.at[0], pr_sem.at[0], partner)
    sign_out = remote(s_ref, sp_v, ps_sem.at[1], pr_sem.at[1], partner)
    ids_out.start()
    sign_out.start()

    def pair_copy(q):
        piece = pl.ds(pl.multiple_of(q * 1024, 1024), 1024)
        return remote(m_ref.at[:, piece], xp_v.at[q], xs_sem.at[q], xr_sem.at[q], partner)

    for q in range(8):
        pair_copy(q).start()

    ids_out.wait_recv()
    mine, other = id_ref[core], idp_v[...]
    left = jnp.where(core == 0, mine, other)
    right = jnp.where(core == 0, other, mine)
    ids_v[chip] = left | ((right ^ (ROWS // 2)) << 16)

    def ids_copy(o):
        to = lax.rem(chip + o, CHIPS)
        return remote(ids_v.at[chip], ids_v.at[chip], is_sem, ir_sem, {"rows": to * 2 + core})

    def ids_send(o, _):
        ids_copy(o).start()
        return 0

    lax.fori_loop(1, CHIPS, ids_send, 0)

    block = lax.broadcasted_iota(I32, (LIST, 128), 0) // KEEP
    parity = block & chip
    for shift in (4, 2, 1):
        parity = parity ^ (parity >> shift)
    sg_v[...] = (1 - 2 * (parity & 1)).astype(F32)

    had = hadamard_rows(2)
    flip = (1 - 2 * core).astype(F32)
    sign_out.wait_recv()

    with jax.named_scope("local transform"):

        def chunk(q, _):
            own_copy(q).wait()
            pair_copy(q).wait_recv()
            own_sign = s_ref[pl.ds(pl.multiple_of(q * 8, 8), 8), :].astype(F32) * flip
            far_sign = sp_v[pl.ds(pl.multiple_of(q * 8, 8), 8), :].astype(F32)
            parts = []
            for i in range(8):
                lanes = slice(i * 128, (i + 1) * 128)
                parts.append(x_v[q, :, lanes] * own_sign[i : i + 1] + xp_v[q, :, lanes] * far_sign[i : i + 1])
            parts = butterflies(parts)
            for p in range(4):
                two = jnp.concatenate([parts[2 * p], parts[2 * p + 1]], 0)
                high = two.astype(BF16)
                low = (two - high.astype(F32)).astype(BF16)
                y_v[q, p] = lax.dot_general(
                    had, jnp.concatenate([high, low], 1), (((1,), (1,)), ((), ())), preferred_element_type=F32
                )
            return 0

        lax.fori_loop(0, 8, chunk, 0)

    pltpu.make_async_copy(ids_v.at[pl.ds(0, CHIPS - 1)], ids_v.at[pl.ds(0, CHIPS - 1)], ir_sem).wait()
    lists = pltpu.make_async_copy(ids_v, ids_s, sm_sem)
    lists.start()

    with jax.named_scope("across chunks"):

        def across(i, _):
            p = i // 4
            for t in range(4):
                row = pl.multiple_of((i % 4) * 32 + t * 8, 8)
                parts = butterflies([y_v[q, p, pl.ds(row, 8), :] for q in range(8)])
                for q in range(8):
                    to = pl.multiple_of(q * 512 + p * 128 + row, 8)
                    t_v[pl.ds(to, 8), :] = parts[q]
                    t_v[pl.ds(to + ROWS // 2, 8), :] = pltpu.roll(parts[q], 64, 1)
            return 0

        lax.fori_loop(0, 16, across, 0)
    lists.wait()

    half = lax.broadcasted_iota(I32, (1, 128), 1) < 64

    def gather(dst, chip_of, pieces, first, count, unroll):
        steps = count // unroll

        def step(i, _):
            piece = i // steps
            start = first + (i - piece * steps) * unroll
            of = chip_of(piece)
            got = []
            for u in range(unroll):
                word = ids_s[of, 0, start + u]
                a = t_v[pl.ds(word & 0xFFFF, 1), :]
                b = t_v[pl.ds(word >> 16, 1), :]
                got.append(jnp.where(half, a, b))
            for u in range(unroll):
                dst[pl.ds(i * unroll + u, 1), :] = got[u]
            return 0

        lax.fori_loop(0, pieces * steps, step, 0)

    count = [0]

    def send(src, dst, device):
        n = count[0]
        count[0] += 1
        copy = remote(src, dst, rs_sem.at[n], rr_sem.at[n], device)
        copy.start()
        return copy

    xp, xm = at(x + 1, z, core), at(x - 1, z, core)
    zp, zm = at(x, z + 1, core), at(x, z - 1, core)
    z_order = (4, 3, -3, 2, -2, 1, -1, 0)
    x_order = (2, 1, -1, 0)

    def chip_at(dx, dz):
        return lax.rem(z + dz + NZ, NZ) * NX + lax.rem(x + dx + NX, NX)

    def pick(order, g, width, n):
        value = jnp.int32(order[g * width])
        for k in range(1, width):
            value = jnp.where(n == k, order[g * width + k], value)
        return value

    sent = []

    a1, a2, az = {}, {}, {}

    def a_one(g):
        for d, first, to in ((0, 0, xp), (1, HA, xm)):
            dst = a1s.at[g, d]
            gather(dst, lambda n: chip_at(2, pick(z_order, g, PA, n)), PA, first, HA, UA)
            for n in range(PA):
                part = pl.ds(n * HA, HA)
                dst[part, :] = dst[part, :] * sg_v[first : first + HA, :]
            a1[g, d] = send(dst, a1r.at[g, d], to)

    def a_two(g):
        for d, dx, first, to in ((0, 1, 0, xp), (1, -1, HA, xm)):
            dst = a2s.at[g, d]
            gather(dst, lambda n: chip_at(dx, pick(z_order, g, PA, n)), PA, 0, RA, UA)
            a1[g, d].wait_recv()
            for n in range(PA):
                with_part = pl.ds(n * RA + first, HA)
                alone = pl.ds(n * RA + HA - first, HA)
                dst[with_part, :] = dst[with_part, :] * sg_v[first : first + HA, :] + a1r[g, d, n * HA : (n + 1) * HA, :]
                dst[alone, :] = dst[alone, :] * sg_v[HA - first : RA - first, :]
            a2[g, d] = send(dst, a2r.at[g, d], to)

    def a_three(g):
        dst = a_sum.at[pl.ds(g * PA * RA, PA * RA)]
        gather(dst, lambda n: chip_at(0, pick(z_order, g, PA, n)), PA, 0, RA, UA)
        a2[g, 0].wait_recv()
        a2[g, 1].wait_recv()
        for n in range(PA):
            part = slice(n * RA, (n + 1) * RA)
            dst[part, :] = dst[part, :] * sg_v[0:RA, :] + (a2r[g, 0, part, :] + a2r[g, 1, part, :])

    def a_z(step):
        if step == 1:
            az[1, 0] = send(a_sum.at[pl.ds(0, HA)], azr.at[0, 0, pl.ds(0, HA)], zp)
            az[1, 1] = send(a_sum.at[pl.ds(HA, HA)], azr.at[1, 0, pl.ds(0, HA)], zm)
            return
        for d, to in ((0, zp), (1, zm)):
            at_row = (2 * step - 3 + d) * RA
            az[step - 1, d].wait_recv()
            if step == 2:
                part = pl.ds(at_row + d * HA, HA)
                a_sum[part, :] = a_sum[part, :] + azr[d, 0, 0:HA, :]
            else:
                part = pl.ds(at_row, RA)
                a_sum[part, :] = a_sum[part, :] + azr[d, step - 2]
            az[step, d] = send(a_sum.at[pl.ds(at_row, RA)], azr.at[d, step - 1], to)

    b1, b2, bx = {}, {}, {}

    def b_one(h):
        for d, first, to in ((0, RA, zp), (1, RA + HB, zm)):
            dst = b1s.at[h, d]
            gather(dst, lambda n: chip_at(pick(x_order, h, PB, n), 4), PB, first, HB, UB)
            for n in range(PB):
                part = pl.ds(n * HB, HB)
                dst[part, :] = dst[part, :] * sg_v[first : first + HB, :]
            b1[h, d] = send(dst, b1r.at[h, d], to)

    def b_next(h, step):
        for d, dz, to in ((0, 5 - step, zp), (1, step - 5, zm)):
            dst = b2s.at[h, d, step - 2]
            gather(dst, lambda n: chip_at(pick(x_order, h, PB, n), dz), PB, RA, RB, UB)
            if step == 2:
                b1[h, d].wait_recv()
                for n in range(PB):
                    first, rest = d * HB, HB - d * HB
                    with_part = pl.ds(n * RB + first, HB)
                    alone = pl.ds(n * RB + rest, HB)
                    dst[with_part, :] = (
                        dst[with_part, :] * sg_v[RA + first : RA + first + HB, :] + b1r[h, d, n * HB : (n + 1) * HB, :]
                    )
                    dst[alone, :] = dst[alone, :] * sg_v[RA + rest : RA + rest + HB, :]
            else:
                b2[h, d, step - 1].wait_recv()
                for n in range(PB):
                    part = slice(n * RB, (n + 1) * RB)
                    dst[part, :] = dst[part, :] * sg_v[RA:LIST, :] + b2r[h, d, step - 3, part, :]
            b2[h, d, step] = send(dst, b2r.at[h, d, step - 2], to)

    def b_five(h):
        dst = b_sum.at[pl.ds(h * PB * RB, PB * RB)]
        gather(dst, lambda n: chip_at(pick(x_order, h, PB, n), 0), PB, RA, RB, UB)
        b2[h, 0, 4].wait_recv()
        b2[h, 1, 4].wait_recv()
        for n in range(PB):
            part = slice(n * RB, (n + 1) * RB)
            dst[part, :] = dst[part, :] * sg_v[RA:LIST, :] + (b2r[h, 0, 2, part, :] + b2r[h, 1, 2, part, :])

    def b_x(step):
        if step == 1:
            bx[1, 0] = send(b_sum.at[pl.ds(0, HB)], bxr.at[0, 0, pl.ds(0, HB)], xp)
            bx[1, 1] = send(b_sum.at[pl.ds(HB, HB)], bxr.at[1, 0, pl.ds(0, HB)], xm)
            return
        for d, to in ((0, xp), (1, xm)):
            at_row = (1 + d) * RB
            bx[1, d].wait_recv()
            part = pl.ds(at_row + d * HB, HB)
            b_sum[part, :] = b_sum[part, :] + bxr[d, 0, 0:HB, :]
            bx[2, d] = send(b_sum.at[pl.ds(at_row, RB)], bxr.at[d, 1], to)

    scale = 1.0 / float(ROWS * CHIPS * 2) ** 0.5
    spread = {}

    def finish(first, rows, total):
        f_v[y, pl.ds(first, rows), :] = total * scale
        src = f_v.at[y, pl.ds(first, rows)]
        for o in range(1, NY):
            spread[first, o] = send(src, src, {"cols": lax.rem(y + o, NY)})
        spread[first, 0] = send(src, fp_v.at[pl.ds(first, rows)], partner)

    def a_finish():
        az[4, 0].wait_recv()
        az[4, 1].wait_recv()
        finish(0, RA, a_sum[7 * RA : 8 * RA, :] + (azr[0, 3] + azr[1, 3]))

    def b_finish():
        bx[2, 0].wait_recv()
        bx[2, 1].wait_recv()
        finish(RA, RB, b_sum[3 * RB : 4 * RB, :] + (bxr[0, 1] + bxr[1, 1]))

    with jax.named_scope("reduce early"):
        b_one(0)
        a_one(0)
        b_one(1)
        a_one(1)
        b_next(0, 2)
        a_two(0)
        a_one(2)
        b_next(1, 2)
    with jax.named_scope("reduce middle"):
        a_two(1)
        b_next(0, 3)
        a_one(3)
        a_three(0)
        a_z(1)
        b_next(1, 3)
        a_two(2)
        b_next(0, 4)
        a_three(1)
        a_z(2)
    with jax.named_scope("reduce late"):
        b_next(1, 4)
        a_two(3)
        a_three(2)
        a_z(3)
        b_five(0)
        b_x(1)
        b_five(1)
        b_x(2)
        a_three(3)
        a_z(4)
    with jax.named_scope("reduce end"):
        b_finish()
        a_finish()

    with jax.named_scope("spread over cols"):
        for first in (RA, 0):
            for o in range(1, NY):
                spread[first, o].wait_recv()
    with jax.named_scope("gram product"):
        mine_t = f_v[y].T
        for c in range(NY):
            whole = jnp.dot(mine_t, f_v[c], precision=lax.Precision.HIGHEST, preferred_element_type=F32)
            p_v[:, c * COLS : (c + 1) * COLS] = whole[:COLS, :COLS] + whole[COLS:, COLS:]

    def corner_copy(src_of, dst, n):
        copies = []
        for o in range(1, 8):
            to = lax.rem(corner + o, 8)
            copies.append(remote(src_of(to), dst, gs_sem.at[n], gr_sem.at[n], at(to // 2, z, lax.rem(to, 2))))
        return copies

    def rows_of(n):
        return pl.ds(pl.multiple_of(n * 8, 8), 8)

    def all_seven(ref, n, sems=gr_sem):
        seven = ref.at[pl.ds(0, 7)]
        pltpu.make_async_copy(seven, seven, sems.at[n]).wait()

    with jax.named_scope("gram rows"):
        first = corner_copy(lambda to: p_v.at[rows_of(to)], g1r.at[corner], 0)
        for copy in first:
            copy.start()
        g1r[corner] = p_v[rows_of(corner), :]
    with jax.named_scope("sketch out"):
        for part in (RA, 0):
            spread[part, 0].wait_recv()
        mine = f_v[y]
        other = fp_v[...]
        even = jnp.where(core == 0, mine, other).reshape(16, 8, 128)
        odd = jnp.where(core == 0, other, mine).reshape(16, 8, 128)
        upper = lax.broadcasted_iota(I32, (16, 8, 128), 1) < 4
        one = jnp.where(upper, even, pltpu.roll(odd, 4, 1))
        two = jnp.where(upper, pltpu.roll(even, 4, 1), odd)
        whole = jnp.stack([one, two], 1).reshape(256, 128).T
        sk_ref[...] = jnp.where(core == 0, whole[:COLS], whole[COLS:])
    with jax.named_scope("gram along z"):
        all_seven(g1r, 0)
        g2r[z] = jnp.sum(g1r[...], 0)
        second = []
        for o in range(1, NZ):
            to = at(x, z + o, core)
            second.append(remote(g2r.at[z], g2r.at[z], gs_sem.at[1], gr_sem.at[1], to))
            second[-1].start()
        all_seven(g2r, 1)
    with jax.named_scope("gram out"):
        g3r[corner] = jnp.sum(g2r[...], 0) * (1.0 / (LIST * 2 * CHIPS * 2))
        third = corner_copy(lambda to: g3r.at[corner], g3r.at[corner], 2)
        for copy in third:
            copy.start()
        all_seven(g3r, 2)
        g_ref[...] = g3r[...].reshape(COLS, NY * COLS)

    with jax.named_scope("drain"):
        ids_out.wait_send()
        sign_out.wait_send()

        def pair_done(q, _):
            pair_copy(q).wait_send()
            return 0

        lax.fori_loop(0, 8, pair_done, 0)

        pltpu.make_async_copy(ids_v.at[pl.ds(0, CHIPS - 1)], ids_v.at[pl.ds(0, CHIPS - 1)], is_sem).wait()
        for group in (a1, a2, az, b1, b2, bx, spread):
            for copy in group.values():
                copy.wait_send()
        for n in range(3):
            all_seven(g1r, n, gs_sem)


MESSAGES = 4 * GA + 8 + 8 * GB + 4 + 8


def on_device(matrix_t, signs, sample_ids):
    row = sample_ids & (ROWS - 1)
    index = ((row >> 7) & 1) * (ROWS // 2) + (row >> 8) * 128 + (row & 127)
    index = index.reshape(CHIPS, 2, KEEP).transpose(1, 0, 2).reshape(2, 1, LIST)
    vm = pltpu.VMEM
    dma = pltpu.SemaphoreType.DMA
    vmem_spec = pl.BlockSpec(memory_space=pltpu.VMEM)
    return pl.pallas_call(
        kernel,
        name="sketch_gram",
        out_shape=(
            jax.ShapeDtypeStruct((COLS, LIST * 2), F32),
            jax.ShapeDtypeStruct((COLS, NY * COLS), F32),
        ),
        in_specs=[pl.BlockSpec(memory_space=pl.ANY), vmem_spec, vmem_spec],
        out_specs=(vmem_spec, vmem_spec),
        scratch_shapes=[
            vm((8, COLS, 1024), F32),
            vm((8, COLS, 1024), F32),
            vm((64, 128), I32),
            vm((8, 4, 128, 128), F32),
            vm((ROWS, 128), F32),
            vm((1, LIST), I32),
            vm((CHIPS, 1, LIST), I32),
            pltpu.SMEM((CHIPS, 1, LIST), I32),
            vm((LIST, 128), F32),
            vm((GA, 2, PA * HA, 128), F32),
            vm((GA, 2, PA * HA, 128), F32),
            vm((GA, 2, PA * RA, 128), F32),
            vm((GA, 2, PA * RA, 128), F32),
            vm((NZ * RA, 128), F32),
            vm((2, 4, RA, 128), F32),
            vm((GB, 2, PB * HB, 128), F32),
            vm((GB, 2, PB * HB, 128), F32),
            vm((GB, 2, 3, PB * RB, 128), F32),
            vm((GB, 2, 3, PB * RB, 128), F32),
            vm((NX * RB, 128), F32),
            vm((2, 2, RB, 128), F32),
            vm((NY, LIST, 128), F32),
            vm((LIST, 128), F32),
            vm((COLS, NY * COLS), F32),
            vm((8, 8, NY * COLS), F32),
            vm((8, 8, NY * COLS), F32),
            vm((8, 8, NY * COLS), F32),
            dma((8,)),
            dma,
            dma((8,)),
            dma((8,)),
            dma((2,)),
            dma((2,)),
            dma,
            dma,
            dma((MESSAGES,)),
            dma((MESSAGES,)),
            dma((3,)),
            dma((3,)),
        ],
        compiler_params=pltpu.CompilerParams(
            collective_id=0, has_side_effects=True, vmem_limit_bytes=40 << 20
        ),
    )(matrix_t, signs.reshape(64, 128), index)


def solution(mesh):
    placed = (P("cols", "rows"), P("rows"), P("rows"))
    return jax.shard_map(
        on_device,
        mesh=mesh,
        in_specs=placed,
        out_specs=(P("cols", "rows"), P("cols", None)),
        check_vma=False,
    )
```

time: 682 us -> 68.1 us (0.10)
  waiting for transfers between devices: 396 us -> 0 us
  blocking collectives: 152 us -> 0 us
  Pallas kernels: 0 us -> 62.7 us
  local copies, waits for them, and re-layouts: 49.9 us -> 3.83 us
  other arithmetic: 40.3 us -> 0.69 us
  matrix products: 18.2 us -> 0 us
  between operations: 14.2 us -> 0.67 us
  starting transfers between devices: 10.9 us -> 0 us
    ppermute x6 -> x0, waiting for transfers between devices: 232 us -> none  [partner_2(): lax.ppermute(shard, axis, [(i, i ^ 1 << distance) for i in range(lax.axis...]
    psum x1 -> x0, waiting for transfers between devices: 165 us -> none  [on_device(): summed = lax.psum(partial_value, 'rows')]
    all_gather x2 -> x0, blocking collectives: 136 us -> none  [the longest x1 125 us: on_device(): every_id = lax.all_gather(sample_ids, 'rows', axis=0, tiled=True)]
    pallas_call x0 -> x1, Pallas kernels: none -> 62.7 us  [on_device(): pl.pallas_call(kernel, name='sketch_gram', out_shape=(jax.ShapeDtypeStruc...]
    select_n x6 -> x0, other arithmetic: 29.3 us -> none  [the longest x5 29.3 us: on_device(): mixed = jnp.where(upper == 1, partner - mixed, mixed + partner)]
    select_n x5 -> x0, local copies, waits for them, and re-layouts: 19.1 us -> none  [on_device(): mixed = jnp.where(upper == 1, partner - mixed, mixed + partner)]
    dot_general x3 -> x0, matrix products: 18.2 us -> none  [the longest x1 8.74 us: on_device(): shaped = jnp.einsum('ab,cbq->caq', sylvester(128), shaped, precision=high)]
    ppermute x6 -> x0, local copies, waits for them, and re-layouts: 17.4 us -> none  [partner_2(): lax.ppermute(shard, axis, [(i, i ^ 1 << distance) for i in range(lax.axis...]
  transfers between devices with their start and end apart: 7 -> 0, of which waited for: 6 -> 0; matrix products, arithmetic and copies ran while one was open for 0% -> 0% of each run, Pallas kernels for 0% -> 0%
where the time goes in v1:
time: 68.1 us; the launch traced here: 67.9 us
  Pallas kernels  62.7 us (92%)
  local copies, waits for them, and re-layouts  3.83 us (6%)
  other arithmetic  0.69 us (1%)
    pallas_call x1, Pallas kernels, on_device(): pl.pallas_call(kernel, name='sketch_gram', out_shape=(jax.ShapeDtypeStruc...  62.7 us
    unnamed x6, local copies, waits for them, and re-layouts  3.61 us

profile of v1, /device:TPU:1, one launch (start us, length us, event | category | flops | bytes accessed | tf_op | source)
XLA Modules:
  0.0 67.9 jit_solution(14712458712425354737)
XLA Ops:
  0.6 0.7 %and_add_fusion = s32[256]{0:T(256)S(1)} fusion(s32[256]{0:T(256)} %param.5), kind=kLoop, calls=%fused_computation | loop fusion | flops 2304 | bytes 2048 | tf_op jit(solution)/shard_map/add | solution.py:458
  1.3 0.1 reshape.14
  1.5 0.1 reshape.15
  1.6 0.0 copy-start
  1.6 1.6 %copy-done = f32[64,8192]{1,0:T(8,128)S(1)} copy-done((f32[64,8192]{1,0:T(8,128)S(1)}, f32[64,8192]{1,0:T(8,128)}, u32[]{:S(2)}) %copy-start) | copy-done | bytes 2097176
  3.2 0.0 copy-start.1
  3.2 0.8 %copy-done.1 = s32[8192]{0:T(1024)S(1)} copy-done((s32[8192]{0:T(1024)S(1)}, s32[8192]{0:T(1024)}, u32[]{:S(2)}) %copy-start.1) | copy-done | bytes 32792
  3.9 62.7 %sketch_gram.1 = (f32[64,256]{1,0:T(8,128)S(1)}, f32[64,256]{1,0:T(8,128)S(1)}) custom-call(f32[64,8192]{1,0:T(8,128)S(1)} %copy-done, s32[64,128]{1,0:T(8,128)S(1)} %bitcast.3, s32[2,1,128]{2,1,0:T(1,128)S(1)} %bitcast.4), custom_call_target="tpu_custom_call" | custom-call | tf_op jit(solution)/shard_map/sketch_gram/pallas_call | solution.py:463
  66.6 0.6 copy.9
  67.3 0.6 copy.10
  (1 shorter events, 0.0 us)
Async XLA Ops:
  1.6 1.6 %copy-start = (f32[64,8192]{1,0:T(8,128)S(1)}, f32[64,8192]{1,0:T(8,128)}, u32[]{:S(2)}) copy-start(f32[64,8192]{1,0:T(8,128)} %m_ref.1) | copy-start | bytes 6291460
  3.2 0.8 %copy-start.1 = (s32[8192]{0:T(1024)S(1)}, s32[8192]{0:T(1024)}, u32[]{:S(2)}) copy-start(s32[8192]{0:T(1024)} %param.4) | copy-start | bytes 98308

commit v2 on v1

v2 whole, which is shorter than its diff:
```python
import jax
import jax.numpy as jnp
from jax import lax
from jax.experimental import pallas as pl
from jax.experimental.pallas import tpu as pltpu
from jax.sharding import PartitionSpec as P

MESH = pl.DeviceIdType.MESH
F32, BF16, I32 = jnp.float32, jnp.bfloat16, jnp.int32

NX, NZ, NY = 4, 8, 4
CHIPS = NX * NZ
COLS, ROWS = 64, 8192
KEEP = 4
LIST = CHIPS * KEEP
RA = 64
HA = RA // 2
RB = LIST - RA
HB = RB // 2
Z_ORDER = (4, 3, -3, 2, -2, 1, -1, 0)
Z_GROUPS = ((0, 1), (1, 2), (3, 2), (5, 2), (7, 1))
X_FAR = (1, -1, 2)
X_ORDER = (2, 1, -1, 0)


def hadamard_rows(copies):
    shape = (128, 128 * copies)
    parity = lax.broadcasted_iota(I32, shape, 0) & lax.broadcasted_iota(I32, shape, 1) & 127
    for shift in (4, 2, 1):
        parity = parity ^ (parity >> shift)
    return (1 - 2 * (parity & 1)).astype(F32).astype(BF16)


def butterflies(parts):
    for stride in (1, 2, 4):
        done = list(parts)
        for i in range(8):
            if not i & stride:
                done[i] = parts[i] + parts[i | stride]
                done[i | stride] = parts[i] - parts[i | stride]
        parts = done
    return parts


def kernel(
    m_ref, s_ref, id_ref, out_ref,
    x_v, xp_v, s_v, sp_v, y_v, t_v, id_v, cls_v, idr_v, ids_v, ids_s, sg_v,
    a1s, a1r, a_sum, a4r, azr,
    b4s, b4r, bs, br, b_sum, bxr,
    f_v, fp_v, p_v, g1r, g2r, g3r,
    lx_sem, sm_sem, xs_sem, xr_sem, ps_sem, pr_sem, is_sem, ir_sem, rs_sem, rr_sem,
    gs_sem, gr_sem,
):
    me, y = lax.axis_index("rows"), lax.axis_index("cols")
    core, chip = me % 2, me // 2
    x, z = chip % NX, chip // NX
    corner = x * 2 + core

    def at(x_to, z_to, core_to):
        return {"rows": (lax.rem(z_to + NZ, NZ) * NX + lax.rem(x_to + NX, NX)) * 2 + core_to}

    partner = at(x, z, 1 - core)

    def remote(src, dst, send, recv, device):
        return pltpu.make_async_remote_copy(
            src_ref=src, dst_ref=dst, send_sem=send, recv_sem=recv, device_id=device, device_id_type=MESH
        )

    barrier = pltpu.get_barrier_semaphore()
    corners = []
    for o in range(1, 8):
        to = lax.rem(corner + o, 8)
        corners.append((to, at(to // 2, z, lax.rem(to, 2))))
    heights = [at(x, z + o, core) for o in range(1, NZ)]
    columns = [{"cols": lax.rem(y + o, NY)} for o in range(1, NY)]
    for device in [device for _, device in corners] + heights + columns:
        pl.semaphore_signal(barrier, inc=1, device_id=device, device_id_type=MESH)

    id_copy = pltpu.make_async_copy(id_ref, id_v, sm_sem.at[0])
    sign_copy = pltpu.make_async_copy(s_ref, s_v, sm_sem.at[1])
    id_copy.start()
    sign_copy.start()

    def own_copy(q):
        piece = pl.ds(pl.multiple_of(q * 1024, 1024), 1024)
        return pltpu.make_async_copy(m_ref.at[:, piece], x_v.at[q], lx_sem.at[q])

    for q in range(8):
        own_copy(q).start()

    id_copy.wait()
    row = id_v[...] & (ROWS - 1)
    place = ((row >> 7) & 1) * (ROWS // 2) + (row >> 8) * 128 + (row & 127)
    place = jnp.concatenate([place, jnp.zeros((6, 128), I32)], 0)
    lane = lax.broadcasted_iota(I32, (8, 128), 1)
    for c in range(2):
        packed = place if c == 0 else pltpu.roll(place, 128 - KEEP, 1)
        for i in range(4):
            packed = jnp.where((lane >> (2 + i)) & 1 == 1, pltpu.roll(packed, 128 - (KEEP << i), 1), packed)
        second = pltpu.roll(packed, 64, 1)
        cls_v[c] = jnp.where(lane[0:1] < 64, packed[0:1], second[1:2])

    pl.semaphore_wait(barrier, len(corners) + len(heights) + len(columns))

    sign_out = remote(s_ref, sp_v, ps_sem, pr_sem, partner)
    sign_out.start()

    def pair_copy(q):
        piece = pl.ds(pl.multiple_of(q * 1024, 1024), 1024)
        return remote(m_ref.at[:, piece], xp_v.at[q], xs_sem.at[q], xr_sem.at[q], partner)

    pair_copy(0).start()

    def wait_all(ref, slots, sem):
        piece = ref.at[pl.ds(0, slots)]
        pltpu.make_async_copy(piece, piece, sem).wait()

    for to, device in corners:
        remote(cls_v.at[lax.rem(to, 2)], idr_v.at[corner], is_sem.at[0], ir_sem.at[0], device).start()
    idr_v[corner] = cls_v[core]
    for q in range(1, 8):
        pair_copy(q).start()

    def lists_along_z():
        wait_all(idr_v, 7, ir_sem.at[0])
        for n in range(NX):
            ids_v[z * NX + n] = idr_v[2 * n] | ((idr_v[2 * n + 1] ^ (ROWS // 2)) << 16)
        four = ids_v.at[pl.ds(z * NX, NX)]
        for device in heights:
            remote(four, four, is_sem.at[1], ir_sem.at[1], device).start()

    block = lax.broadcasted_iota(I32, (LIST, 128), 0) // KEEP
    parity = block & chip
    for shift in (4, 2, 1):
        parity = parity ^ (parity >> shift)
    sg_v[...] = (1 - 2 * (parity & 1)).astype(F32)

    had = hadamard_rows(2)
    flip = (1 - 2 * core).astype(F32)
    sign_copy.wait()
    sign_out.wait_recv()

    with jax.named_scope("local transform"):

        def chunk(q, _):
            own_copy(q).wait()
            pair_copy(q).wait_recv()
            own_sign = s_v[pl.ds(pl.multiple_of(q * 8, 8), 8), :].astype(F32) * flip
            far_sign = sp_v[pl.ds(pl.multiple_of(q * 8, 8), 8), :].astype(F32)
            parts = []
            for i in range(8):
                lanes = slice(i * 128, (i + 1) * 128)
                parts.append(x_v[q, :, lanes] * own_sign[i : i + 1] + xp_v[q, :, lanes] * far_sign[i : i + 1])
            parts = butterflies(parts)
            for p in range(4):
                two = jnp.concatenate([parts[2 * p], parts[2 * p + 1]], 0)
                high = two.astype(BF16)
                low = (two - high.astype(F32)).astype(BF16)
                y_v[q, p] = lax.dot_general(
                    had, jnp.concatenate([high, low], 1), (((1,), (1,)), ((), ())), preferred_element_type=F32
                )
            return 0

        lax.fori_loop(0, 4, chunk, 0)
        lists_along_z()
        lax.fori_loop(4, 8, chunk, 0)

    with jax.named_scope("across chunks"):

        def across(i, _):
            p = i // 4
            for t in range(4):
                row = pl.multiple_of((i % 4) * 32 + t * 8, 8)
                parts = butterflies([y_v[q, p, pl.ds(row, 8), :] for q in range(8)])
                for q in range(8):
                    to = pl.multiple_of(q * 512 + p * 128 + row, 8)
                    t_v[pl.ds(to, 8), :] = parts[q]
                    t_v[pl.ds(to + ROWS // 2, 8), :] = pltpu.roll(parts[q], 64, 1)
            return 0

        lax.fori_loop(0, 16, across, 0)
    wait_all(ids_v, 7 * NX, ir_sem.at[1])
    lists = pltpu.make_async_copy(ids_v, ids_s, sm_sem.at[2])
    lists.start()
    lists.wait()

    half = lax.broadcasted_iota(I32, (1, 128), 1) < 64

    def gather(dst, at_row, of, first, rows):
        for start in range(first, first + rows, 32):
            got = []
            for j in range(start, start + 32):
                if j % KEEP == 0:
                    sign = sg_v[j : j + 1, :]
                word = ids_s[of, 0, j]
                a = t_v[pl.ds(word & 0xFFFF, 1), :]
                b = t_v[pl.ds(word >> 16, 1), :]
                got.append(jnp.where(half, a, b) * sign)
            for u in range(32):
                dst[pl.ds(at_row + (start - first + u), 1), :] = got[u]

    count = [0]

    def send(src, dst, device):
        n = count[0]
        count[0] += 1
        copy = remote(src, dst, rs_sem.at[n], rr_sem.at[n], device)
        copy.start()
        return copy

    ups = (at(x, z + 1, core), at(x, z - 1, core))
    twos = (at(x, z + 2, core), at(x, z - 2, core))

    def chip_at(dx, dz):
        return lax.rem(z + dz + NZ, NZ) * NX + lax.rem(x + dx + NX, NX)

    def pick(values, n):
        value = jnp.int32(values[0])
        for k in range(1, len(values)):
            value = jnp.where(n == k, values[k], value)
        return value

    a1, az = {}, {}

    def a_send(g):
        place, width = Z_GROUPS[g]

        def one(n, _):
            slot = n // width
            dz = pick(Z_ORDER[place : place + width], n - slot * width)
            at_row = pl.multiple_of((slot * (NZ - width) + place + n) * RA, RA)
            gather(a1s, at_row, chip_at(pick(X_FAR, slot), dz), 0, RA)
            return 0

        lax.fori_loop(0, 3 * width, one, 0)
        for slot in range(3):
            part = pl.ds((slot * NZ + place) * RA, width * RA)
            a1[g, slot] = send(a1s.at[part], a1r.at[part], at(x + X_FAR[slot], z, core))

    def a_own(g):
        place, width = Z_GROUPS[g]

        def one(n, _):
            at_row = pl.multiple_of((place + n) * RA, RA)
            gather(a_sum, at_row, chip_at(0, pick(Z_ORDER[place : place + width], n)), 0, RA)
            return 0

        lax.fori_loop(0, width, one, 0)

    def a_add(g):
        place, width = Z_GROUPS[g]
        total = a_sum[place * RA : (place + width) * RA, :]
        for slot in range(3):
            a1[g, slot].wait_recv()
            total = total + a1r[(slot * NZ + place) * RA : (slot * NZ + place + width) * RA, :]
        a_sum[place * RA : (place + width) * RA, :] = total

    def a_z(step):
        for d in range(2):
            if step == 4:
                az[4, d] = send(a_sum.at[pl.ds(d * HA, HA)], a4r.at[d], twos[d])
                continue
            at_row = (7 - 2 * step + d) * RA
            if step == 2:
                az[4, d].wait_recv()
                part = pl.ds(at_row + d * HA, HA)
                a_sum[part, :] = a_sum[part, :] + a4r[d]
            if step < 3:
                az[step + 1, d].wait_recv()
                part = pl.ds(at_row, RA)
                a_sum[part, :] = a_sum[part, :] + azr[step, d]
            az[step, d] = send(a_sum.at[pl.ds(at_row, RA)], azr.at[step - 1, d], ups[d])

    b4, bz, bx = {}, {}, {}

    def b_far():
        def one(h, _):
            gather(b4s, pl.multiple_of(h * RB, RB), chip_at(pick(X_ORDER, h), 4), RA, RB)
            return 0

        lax.fori_loop(0, NX, one, 0)
        for h in range(NX):
            for d in range(2):
                b4[h, d] = send(b4s.at[pl.ds(h * RB + d * HB, HB)], b4r.at[h, d], twos[d])

    def b_own(step, first, last):
        def one(n, _):
            d = lax.rem(n, 2)
            h = n // 2
            dst = bs.at[step - 1, h, d]
            gather(dst, 0, chip_at(pick(X_ORDER, h), step - 2 * step * d), RA, RB)
            return 0

        lax.fori_loop(2 * first, 2 * last, one, 0)

    def b_z(step, h):
        for d in range(2):
            src = bs.at[step - 1, h, d]
            if step == 2:
                b4[h, d].wait_recv()
                part = pl.ds(d * HB, HB)
                src[part, :] = src[part, :] + b4r[h, d]
            if step < 3:
                bz[step + 1, h, d].wait_recv()
                src[...] = src[...] + br[step, h, d]
            bz[step, h, d] = send(src, br.at[step - 1, h, d], ups[d])

    def b_home():
        def one(h, _):
            gather(b_sum, pl.multiple_of(h * RB, RB), chip_at(pick(X_ORDER, h), 0), RA, RB)
            return 0

        lax.fori_loop(0, NX, one, 0)

    def b_x(h):
        part = pl.ds(h * RB, RB)
        bz[1, h, 0].wait_recv()
        bz[1, h, 1].wait_recv()
        b_sum[part, :] = b_sum[part, :] + (br[0, h, 0] + br[0, h, 1])
        if X_ORDER[h]:
            bx[h] = send(b_sum.at[part], bxr.at[h], at(x + X_ORDER[h], z, core))

    scale = 1.0 / float(ROWS * CHIPS * 2) ** 0.5
    spread = {}

    def finish(first, rows, total):
        f_v[y, pl.ds(first, rows), :] = total * scale
        src = f_v.at[y, pl.ds(first, rows)]
        for o in range(1, NY):
            spread[first, o] = send(src, src, columns[o - 1])
        spread[first, 0] = send(src, fp_v.at[pl.ds(first, rows)], partner)

    def a_finish():
        az[1, 0].wait_recv()
        az[1, 1].wait_recv()
        finish(0, RA, a_sum[7 * RA : 8 * RA, :] + (azr[0, 0] + azr[0, 1]))

    def b_finish():
        total = b_sum[3 * RB : 4 * RB, :]
        for h in range(3):
            bx[h].wait_recv()
            total = total + bxr[h]
        finish(RA, RB, total)

    with jax.named_scope("reduce early"):
        b_far()
        a_send(0)
        b_own(3, 0, 2)
        b_z(3, 0)
        b_z(3, 1)
        b_own(3, 2, 4)
        b_z(3, 2)
        b_z(3, 3)
        a_send(1)
        b_own(2, 0, 4)
        a_own(0)
        a_send(2)
    with jax.named_scope("reduce middle"):
        b_z(2, 0)
        b_z(2, 1)
        a_add(0)
        a_z(4)
        b_z(2, 2)
        b_z(2, 3)
        a_send(3)
        b_own(1, 0, 4)
        a_own(1)
        a_add(1)
        a_z(3)
        a_send(4)
        a_own(2)
        b_z(1, 0)
        b_z(1, 1)
        b_z(1, 2)
        b_z(1, 3)
    with jax.named_scope("reduce late"):
        b_home()
        a_own(3)
        a_own(4)
        a_add(2)
        a_z(2)
        b_x(0)
        b_x(1)
        b_x(2)
        b_x(3)
        a_add(3)
        a_z(1)
        a_add(4)
    with jax.named_scope("reduce end"):
        b_finish()
        a_finish()

    with jax.named_scope("spread over cols"):
        for first in (RA, 0):
            for o in range(1, NY):
                spread[first, o].wait_recv()
    with jax.named_scope("gram product"):
        mine_t = f_v[y].T
        for c in range(NY):
            whole = jnp.dot(mine_t, f_v[c], precision=lax.Precision.HIGHEST, preferred_element_type=F32)
            p_v[:, c * COLS : (c + 1) * COLS] = whole[:COLS, :COLS] + whole[COLS:, COLS:]

    def corner_copy(src_of, dst, n):
        return [remote(src_of(to), dst, gs_sem.at[n], gr_sem.at[n], device) for to, device in corners]

    def rows_of(n):
        return pl.ds(pl.multiple_of(n * 8, 8), 8)

    def all_seven(ref, n, sems=gr_sem):
        seven = ref.at[pl.ds(0, 7)]
        pltpu.make_async_copy(seven, seven, sems.at[n]).wait()

    with jax.named_scope("gram rows"):
        first = corner_copy(lambda to: p_v.at[rows_of(to)], g1r.at[corner], 0)
        for copy in first:
            copy.start()
        g1r[corner] = p_v[rows_of(corner), :]
    with jax.named_scope("drain"):
        sign_out.wait_send()

        def pair_done(q, _):
            pair_copy(q).wait_send()
            return 0

        lax.fori_loop(0, 8, pair_done, 0)

        wait_all(idr_v, 7, is_sem.at[0])
        wait_all(ids_v, 7 * NX, is_sem.at[1])
        for group in (a1, az, b4, bz, bx):
            for copy in group.values():
                copy.wait_send()
    with jax.named_scope("sketch out"):
        for part in (RA, 0):
            spread[part, 0].wait_recv()
        mine = f_v[y]
        other = fp_v[...]
        even = jnp.where(core == 0, mine, other).reshape(16, 8, 128)
        odd = jnp.where(core == 0, other, mine).reshape(16, 8, 128)
        upper = lax.broadcasted_iota(I32, (16, 8, 128), 1) < 4
        one = jnp.where(upper, even, pltpu.roll(odd, 4, 1))
        two = jnp.where(upper, pltpu.roll(even, 4, 1), odd)
        whole = jnp.stack([one, two], 1).reshape(256, 128).T
        out_ref[:COLS, :] = jnp.where(core == 0, whole[:COLS], whole[COLS:])
    with jax.named_scope("gram along z"):
        all_seven(g1r, 0)
        g2r[z] = jnp.sum(g1r[...], 0)
        second = []
        for device in heights:
            second.append(remote(g2r.at[z], g2r.at[z], gs_sem.at[1], gr_sem.at[1], device))
            second[-1].start()
        all_seven(g2r, 1)
    with jax.named_scope("gram out"):
        g3r[corner] = jnp.sum(g2r[...], 0)
        third = corner_copy(lambda to: g3r.at[corner], g3r.at[corner], 2)
        for copy in third:
            copy.start()
        all_seven(g3r, 2)
        out_ref[COLS:, :] = g3r[...].reshape(COLS, NY * COLS)

    for copy in spread.values():
        copy.wait_send()
    for n in range(3):
        all_seven(g1r, n, gs_sem)


MESSAGES = 15 + 8 + 8 + 24 + 3 + 8


def on_device(matrix_t, signs, sample_ids):
    vm = pltpu.VMEM
    dma = pltpu.SemaphoreType.DMA
    vmem_spec = pl.BlockSpec(memory_space=pltpu.VMEM)
    operands = matrix_t, signs.reshape(64, 128), sample_ids.reshape(2, 128)
    both = pl.pallas_call(
        kernel,
        name="sketch_gram",
        out_shape=jax.ShapeDtypeStruct((2 * COLS, NY * COLS), F32),
        in_specs=[pl.BlockSpec(memory_space=pl.ANY)] * 3,
        out_specs=vmem_spec,
        scratch_shapes=[
            vm((8, COLS, 1024), F32),
            vm((8, COLS, 1024), F32),
            vm((64, 128), I32),
            vm((64, 128), I32),
            vm((8, 4, 128, 128), F32),
            vm((ROWS, 128), F32),
            vm((2, 128), I32),
            vm((2, 1, LIST), I32),
            vm((8, 1, LIST), I32),
            vm((CHIPS, 1, LIST), I32),
            pltpu.SMEM((CHIPS, 1, LIST), I32),
            vm((LIST, 128), F32),
            vm((3 * NZ * RA, 128), F32),
            vm((3 * NZ * RA, 128), F32),
            vm((NZ * RA, 128), F32),
            vm((2, HA, 128), F32),
            vm((3, 2, RA, 128), F32),
            vm((NX * RB, 128), F32),
            vm((NX, 2, HB, 128), F32),
            vm((3, NX, 2, RB, 128), F32),
            vm((3, NX, 2, RB, 128), F32),
            vm((NX * RB, 128), F32),
            vm((3, RB, 128), F32),
            vm((NY, LIST, 128), F32),
            vm((LIST, 128), F32),
            vm((COLS, NY * COLS), F32),
            vm((8, 8, NY * COLS), F32),
            vm((8, 8, NY * COLS), F32),
            vm((8, 8, NY * COLS), F32),
            dma((8,)),
            dma((3,)),
            dma((8,)),
            dma((8,)),
            dma,
            dma,
            dma((2,)),
            dma((2,)),
            dma((MESSAGES,)),
            dma((MESSAGES,)),
            dma((3,)),
            dma((3,)),
        ],
        compiler_params=pltpu.CompilerParams(
            collective_id=0, has_side_effects=True, vmem_limit_bytes=40 << 20
        ),
    )(*(pltpu.with_memory_space_constraint(v, pltpu.HBM) for v in operands))
    return both[:COLS], both[COLS:] * (1.0 / (LIST * 2 * CHIPS * 2))


def solution(mesh):
    placed = (P("cols", "rows"), P("rows"), P("rows"))
    return jax.shard_map(
        on_device,
        mesh=mesh,
        in_specs=placed,
        out_specs=(P("cols", "rows"), P("cols", None)),
        check_vma=False,
    )
```

time: 68.1 us -> 59.7 us (0.88)
  Pallas kernels: 62.7 us -> 58.3 us
  local copies, waits for them, and re-layouts: 3.83 us -> 0 us
    pallas_call x1, Pallas kernels: 62.7 us -> 58.3 us  [on_device(): pl.pallas_call(kernel, name='sketch_gram', out_shape=jax.ShapeDtypeStruct...]
    unnamed x6 -> x0, local copies, waits for them, and re-layouts: 3.61 us -> none
    add x1 -> x0, other arithmetic: 0.69 us -> none  [on_device(): index = (row >> 7 & 1) * (ROWS // 2) + (row >> 8) * 128 + (row & 127)]
where the time goes in v2:
time: 59.7 us; the launch traced here: 59.5 us
  Pallas kernels  58.3 us (98%)
  other arithmetic  0.66 us (1%)
  between operations  0.64 us (1%)
    pallas_call x1, Pallas kernels, on_device(): pl.pallas_call(kernel, name='sketch_gram', out_shape=jax.ShapeDtypeStruct...  58.3 us

profile of v2, /device:TPU:1, one launch (start us, length us, event | category | flops | bytes accessed | tf_op | source)
XLA Modules:
  0.0 59.5 jit_solution(11960257792528574968)
XLA Ops:
  0.6 58.3 %sketch_gram.1 = f32[128,256]{1,0:T(8,128)S(1)} custom-call(f32[64,8192]{1,0:T(8,128)} %m_ref.1, s32[64,128]{1,0:T(8,128)} %bitcast.2, s32[2,128]{1,0:T(2,128)} %bitcast.3), custom_call_target="tpu_custom_call" | custom-call | tf_op jit(solution)/shard_map/sketch_gram/pallas_call | solution.py:474
  58.9 0.7 %slice_multiply_fusion = (f32[64,256]{1,0:T(8,128)}, f32[64,256]{1,0:T(8,128)}) fusion(f32[128,256]{1,0:T(8,128)S(1)} %sketch_gram.1), kind=kLoop, calls=%fused_computation | loop fusion | flops 16384 | bytes 262144 | tf_op jit(solution)/shard_map/mul | solution.py:527

commit v3 on v2

--- a/solution.py
+++ b/solution.py
@@ -13,13 +13,14 @@
 COLS, ROWS = 64, 8192
 KEEP = 4
 LIST = CHIPS * KEEP
-RA = 64
+RA = 80
 HA = RA // 2
 RB = LIST - RA
 HB = RB // 2
 Z_ORDER = (4, 3, -3, 2, -2, 1, -1, 0)
 Z_GROUPS = ((0, 1), (1, 2), (3, 2), (5, 2), (7, 1))
-X_FAR = (1, -1, 2)
+F_GROUPS = ((0, 3), (3, 5))
+UNROLL = {RA: 40, HA: 40, RB: 48}
 X_ORDER = (2, 1, -1, 0)
 
 
@@ -45,7 +46,7 @@
 def kernel(
     m_ref, s_ref, id_ref, out_ref,
     x_v, xp_v, s_v, sp_v, y_v, t_v, id_v, cls_v, idr_v, ids_v, ids_s, sg_v,
-    a1s, a1r, a_sum, a4r, azr,
+    afs, afr, ans, anr, a_sum, a4r, azr,
     b4s, b4r, bs, br, b_sum, bxr,
     f_v, fp_v, p_v, g1r, g2r, g3r,
     lx_sem, sm_sem, xs_sem, xr_sem, ps_sem, pr_sem, is_sem, ir_sem, rs_sem, rr_sem,
@@ -187,16 +188,17 @@
     half = lax.broadcasted_iota(I32, (1, 128), 1) < 64
 
     def gather(dst, at_row, of, first, rows):
-        for start in range(first, first + rows, 32):
+        unroll = UNROLL[rows]
+        for start in range(first, first + rows, unroll):
             got = []
-            for j in range(start, start + 32):
-                if j % KEEP == 0:
+            for j in range(start, start + unroll):
+                if j == start or j % KEEP == 0:
                     sign = sg_v[j : j + 1, :]
                 word = ids_s[of, 0, j]
                 a = t_v[pl.ds(word & 0xFFFF, 1), :]
                 b = t_v[pl.ds(word >> 16, 1), :]
                 got.append(jnp.where(half, a, b) * sign)
-            for u in range(32):
+            for u in range(unroll):
                 dst[pl.ds(at_row + (start - first + u), 1), :] = got[u]
 
     count = [0]
@@ -220,40 +222,59 @@
             value = jnp.where(n == k, values[k], value)
         return value
 
-    a1, az = {}, {}
-
-    def a_send(g):
+    sides = (at(x + 1, z, core), at(x - 1, z, core))
+    af, an, az = {}, {}, {}
+
+    def a_far(g):
+        place, width = F_GROUPS[g]
+
+        def one(n, _):
+            chip_to = chip_at(2, pick(Z_ORDER[place : place + width], n))
+            at_row = pl.multiple_of((place + n) * HA, HA)
+            gather(afs.at[0], at_row, chip_to, 0, HA)
+            gather(afs.at[1], at_row, chip_to, HA, HA)
+            return 0
+
+        lax.fori_loop(0, width, one, 0)
+        part = pl.ds(place * HA, width * HA)
+        for d in range(2):
+            af[g, d] = send(afs.at[d, part], afr.at[d, part], sides[d])
+
+    def a_near(place, last):
+        def one(n, _):
+            d = lax.rem(n, 2)
+            k = n // 2
+            at_row = pl.multiple_of(k * RA, RA)
+            gather(ans.at[d], at_row, chip_at(1 - 2 * d, pick(Z_ORDER, k)), 0, RA)
+            return 0
+
+        lax.fori_loop(2 * place, 2 * last, one, 0)
+
+    def a_x(g):
         place, width = Z_GROUPS[g]
-
+        part = pl.ds(place * RA, width * RA)
+        for d in range(2):
+            for f in range(2):
+                if F_GROUPS[f][0] == place:
+                    af[f, d].wait_recv()
+            for k in range(place, place + width):
+                rows = pl.ds(k * RA + d * HA, HA)
+                ans[d, rows, :] = ans[d, rows, :] + afr[d, k * HA : (k + 1) * HA, :]
+            an[g, d] = send(ans.at[d, part], anr.at[d, part], sides[d])
+
+    def a_own():
         def one(n, _):
-            slot = n // width
-            dz = pick(Z_ORDER[place : place + width], n - slot * width)
-            at_row = pl.multiple_of((slot * (NZ - width) + place + n) * RA, RA)
-            gather(a1s, at_row, chip_at(pick(X_FAR, slot), dz), 0, RA)
-            return 0
-
-        lax.fori_loop(0, 3 * width, one, 0)
-        for slot in range(3):
-            part = pl.ds((slot * NZ + place) * RA, width * RA)
-            a1[g, slot] = send(a1s.at[part], a1r.at[part], at(x + X_FAR[slot], z, core))
-
-    def a_own(g):
-        place, width = Z_GROUPS[g]
-
-        def one(n, _):
-            at_row = pl.multiple_of((place + n) * RA, RA)
-            gather(a_sum, at_row, chip_at(0, pick(Z_ORDER[place : place + width], n)), 0, RA)
-            return 0
-
-        lax.fori_loop(0, width, one, 0)
+            gather(a_sum, pl.multiple_of(n * RA, RA), chip_at(0, pick(Z_ORDER, n)), 0, RA)
+            return 0
+
+        lax.fori_loop(0, NZ, one, 0)
 
     def a_add(g):
         place, width = Z_GROUPS[g]
-        total = a_sum[place * RA : (place + width) * RA, :]
-        for slot in range(3):
-            a1[g, slot].wait_recv()
-            total = total + a1r[(slot * NZ + place) * RA : (slot * NZ + place + width) * RA, :]
-        a_sum[place * RA : (place + width) * RA, :] = total
+        an[g, 0].wait_recv()
+        an[g, 1].wait_recv()
+        part = slice(place * RA, (place + width) * RA)
+        a_sum[part, :] = a_sum[part, :] + (anr[0, part, :] + anr[1, part, :])
 
     def a_z(step):
         for d in range(2):
@@ -265,11 +286,11 @@
                 az[4, d].wait_recv()
                 part = pl.ds(at_row + d * HA, HA)
                 a_sum[part, :] = a_sum[part, :] + a4r[d]
-            if step < 3:
-                az[step + 1, d].wait_recv()
+                az[3, d].wait_recv()
                 part = pl.ds(at_row, RA)
-                a_sum[part, :] = a_sum[part, :] + azr[step, d]
-            az[step, d] = send(a_sum.at[pl.ds(at_row, RA)], azr.at[step - 1, d], ups[d])
+                a_sum[part, :] = a_sum[part, :] + azr[2, d]
+            to = twos[d] if step == 2 else ups[d]
+            az[step, d] = send(a_sum.at[pl.ds(at_row, RA)], azr.at[step - 1, d], to)
 
     b4, bz, bx = {}, {}, {}
 
@@ -331,9 +352,12 @@
         spread[first, 0] = send(src, fp_v.at[pl.ds(first, rows)], partner)
 
     def a_finish():
-        az[1, 0].wait_recv()
-        az[1, 1].wait_recv()
-        finish(0, RA, a_sum[7 * RA : 8 * RA, :] + (azr[0, 0] + azr[0, 1]))
+        total = a_sum[7 * RA : 8 * RA, :]
+        for step in (1, 2):
+            az[step, 0].wait_recv()
+            az[step, 1].wait_recv()
+            total = total + (azr[step - 1, 0] + azr[step - 1, 1])
+        finish(0, RA, total)
 
     def b_finish():
         total = b_sum[3 * RB : 4 * RB, :]
@@ -344,47 +368,47 @@
 
     with jax.named_scope("reduce early"):
         b_far()
-        a_send(0)
+        a_far(0)
         b_own(3, 0, 2)
         b_z(3, 0)
         b_z(3, 1)
+        a_far(1)
         b_own(3, 2, 4)
         b_z(3, 2)
         b_z(3, 3)
-        a_send(1)
+        a_near(0, 3)
         b_own(2, 0, 4)
-        a_own(0)
-        a_send(2)
     with jax.named_scope("reduce middle"):
+        a_x(0)
+        a_x(1)
         b_z(2, 0)
         b_z(2, 1)
+        b_z(2, 2)
+        b_z(2, 3)
+        a_near(3, 8)
+        a_x(2)
+        a_x(3)
+        a_x(4)
+        b_own(1, 0, 4)
+        a_own()
+    with jax.named_scope("reduce late"):
         a_add(0)
         a_z(4)
-        b_z(2, 2)
-        b_z(2, 3)
-        a_send(3)
-        b_own(1, 0, 4)
-        a_own(1)
+        b_z(1, 0)
+        b_z(1, 1)
         a_add(1)
         a_z(3)
-        a_send(4)
-        a_own(2)
-        b_z(1, 0)
-        b_z(1, 1)
         b_z(1, 2)
         b_z(1, 3)
-    with jax.named_scope("reduce late"):
         b_home()
-        a_own(3)
-        a_own(4)
         a_add(2)
         a_z(2)
         b_x(0)
         b_x(1)
+        a_add(3)
+        a_z(1)
         b_x(2)
         b_x(3)
-        a_add(3)
-        a_z(1)
         a_add(4)
     with jax.named_scope("reduce end"):
         b_finish()
@@ -426,7 +450,7 @@
 
         wait_all(idr_v, 7, is_sem.at[0])
         wait_all(ids_v, 7 * NX, is_sem.at[1])
-        for group in (a1, az, b4, bz, bx):
+        for group in (af, an, az, b4, bz, bx):
             for copy in group.values():
                 copy.wait_send()
     with jax.named_scope("sketch out"):
@@ -463,7 +487,7 @@
         all_seven(g1r, n, gs_sem)
 
 
-MESSAGES = 15 + 8 + 8 + 24 + 3 + 8
+MESSAGES = 4 + 10 + 8 + 8 + 24 + 3 + 8
 
 
 def on_device(matrix_t, signs, sample_ids):
@@ -490,8 +514,10 @@
             vm((CHIPS, 1, LIST), I32),
             pltpu.SMEM((CHIPS, 1, LIST), I32),
             vm((LIST, 128), F32),
-            vm((3 * NZ * RA, 128), F32),
-            vm((3 * NZ * RA, 128), F32),
+            vm((2, NZ * HA, 128), F32),
+            vm((2, NZ * HA, 128), F32),
+            vm((2, NZ * RA, 128), F32),
+            vm((2, NZ * RA, 128), F32),
             vm((NZ * RA, 128), F32),
             vm((2, HA, 128), F32),
             vm((3, 2, RA, 128), F32),

time: 59.7 us -> 59.4 us (level)
  no operation moved by 1% of the time
where the time goes in v3:
time: 59.4 us; the launch traced here: 59.3 us
  Pallas kernels  58 us (98%)
  other arithmetic  0.66 us (1%)
  between operations  0.64 us (1%)
    pallas_call x1, Pallas kernels, on_device(): pl.pallas_call(kernel, name='sketch_gram', out_shape=jax.ShapeDtypeStruct...  58 us

profile of v3, /device:TPU:1, one launch (start us, length us, event | category | flops | bytes accessed | tf_op | source)
XLA Modules:
  0.0 59.3 jit_solution(1338020008084062117)
XLA Ops:
  0.6 58.0 %sketch_gram.1 = f32[128,256]{1,0:T(8,128)S(1)} custom-call(f32[64,8192]{1,0:T(8,128)} %m_ref.1, s32[64,128]{1,0:T(8,128)} %bitcast.2, s32[2,128]{1,0:T(2,128)} %bitcast.3), custom_call_target="tpu_custom_call" | custom-call | tf_op jit(solution)/shard_map/sketch_gram/pallas_call | solution.py:498
  58.6 0.7 %slice_multiply_fusion = (f32[64,256]{1,0:T(8,128)}, f32[64,256]{1,0:T(8,128)}) fusion(f32[128,256]{1,0:T(8,128)S(1)} %sketch_gram.1), kind=kLoop, calls=%fused_computation | loop fusion | flops 16384 | bytes 262144 | tf_op jit(solution)/shard_map/mul | solution.py:553

commit v4 on v3

--- a/solution.py
+++ b/solution.py
@@ -14,13 +14,13 @@
 KEEP = 4
 LIST = CHIPS * KEEP
 RA = 80
-HA = RA // 2
 RB = LIST - RA
-HB = RB // 2
+A_HALF = (-(-RA // 16) * 8, RA - -(-RA // 16) * 8)
+B_HALF = (-(-RB // 16) * 8, RB - -(-RB // 16) * 8)
+A_FROM, B_FROM = (0, A_HALF[0]), (0, B_HALF[0])
 Z_ORDER = (4, 3, -3, 2, -2, 1, -1, 0)
 Z_GROUPS = ((0, 1), (1, 2), (3, 2), (5, 2), (7, 1))
-F_GROUPS = ((0, 3), (3, 5))
-UNROLL = {RA: 40, HA: 40, RB: 48}
+F_GROUPS = ((0, 1), (1, 2), (3, 5))
 X_ORDER = (2, 1, -1, 0)
 
 
@@ -50,7 +50,7 @@
     b4s, b4r, bs, br, b_sum, bxr,
     f_v, fp_v, p_v, g1r, g2r, g3r,
     lx_sem, sm_sem, xs_sem, xr_sem, ps_sem, pr_sem, is_sem, ir_sem, rs_sem, rr_sem,
-    gs_sem, gr_sem,
+    gs_sem, gr_sem, far_sem,
 ):
     me, y = lax.axis_index("rows"), lax.axis_index("cols")
     core, chip = me % 2, me // 2
@@ -74,7 +74,8 @@
         corners.append((to, at(to // 2, z, lax.rem(to, 2))))
     heights = [at(x, z + o, core) for o in range(1, NZ)]
     columns = [{"cols": lax.rem(y + o, NY)} for o in range(1, NY)]
-    for device in [device for _, device in corners] + heights + columns:
+    close = [at(x, z + o, core) for o in (1, 2, -1, -2)]
+    for device in [device for _, device in corners] + close + columns:
         pl.semaphore_signal(barrier, inc=1, device_id=device, device_id_type=MESH)
 
     id_copy = pltpu.make_async_copy(id_ref, id_v, sm_sem.at[0])
@@ -101,7 +102,9 @@
         second = pltpu.roll(packed, 64, 1)
         cls_v[c] = jnp.where(lane[0:1] < 64, packed[0:1], second[1:2])
 
-    pl.semaphore_wait(barrier, len(corners) + len(heights) + len(columns))
+    pl.semaphore_wait(barrier, len(corners) + len(close) + len(columns))
+    for o in (2, -2):
+        pl.semaphore_signal(far_sem, inc=1, device_id=at(x, z + o, core), device_id_type=MESH)
 
     sign_out = remote(s_ref, sp_v, ps_sem, pr_sem, partner)
     sign_out.start()
@@ -123,6 +126,7 @@
         pair_copy(q).start()
 
     def lists_along_z():
+        pl.semaphore_wait(far_sem, 2)
         wait_all(idr_v, 7, ir_sem.at[0])
         for n in range(NX):
             ids_v[z * NX + n] = idr_v[2 * n] | ((idr_v[2 * n + 1] ^ (ROWS // 2)) << 16)
@@ -188,7 +192,7 @@
     half = lax.broadcasted_iota(I32, (1, 128), 1) < 64
 
     def gather(dst, at_row, of, first, rows):
-        unroll = UNROLL[rows]
+        unroll = rows if rows <= 48 else rows // 2
         for start in range(first, first + rows, unroll):
             got = []
             for j in range(start, start + unroll):
@@ -230,14 +234,14 @@
 
         def one(n, _):
             chip_to = chip_at(2, pick(Z_ORDER[place : place + width], n))
-            at_row = pl.multiple_of((place + n) * HA, HA)
-            gather(afs.at[0], at_row, chip_to, 0, HA)
-            gather(afs.at[1], at_row, chip_to, HA, HA)
+            for d in range(2):
+                at_row = pl.multiple_of((place + n) * A_HALF[d], 8)
+                gather(afs.at[d], at_row, chip_to, A_FROM[d], A_HALF[d])
             return 0
 
         lax.fori_loop(0, width, one, 0)
-        part = pl.ds(place * HA, width * HA)
         for d in range(2):
+            part = pl.ds(place * A_HALF[d], width * A_HALF[d])
             af[g, d] = send(afs.at[d, part], afr.at[d, part], sides[d])
 
     def a_near(place, last):
@@ -254,12 +258,12 @@
         place, width = Z_GROUPS[g]
         part = pl.ds(place * RA, width * RA)
         for d in range(2):
-            for f in range(2):
+            for f in range(3):
                 if F_GROUPS[f][0] == place:
                     af[f, d].wait_recv()
             for k in range(place, place + width):
-                rows = pl.ds(k * RA + d * HA, HA)
-                ans[d, rows, :] = ans[d, rows, :] + afr[d, k * HA : (k + 1) * HA, :]
+                rows = pl.ds(k * RA + A_FROM[d], A_HALF[d])
+                ans[d, rows, :] = ans[d, rows, :] + afr[d, k * A_HALF[d] : (k + 1) * A_HALF[d], :]
             an[g, d] = send(ans.at[d, part], anr.at[d, part], sides[d])
 
     def a_own():
@@ -279,13 +283,13 @@
     def a_z(step):
         for d in range(2):
             if step == 4:
-                az[4, d] = send(a_sum.at[pl.ds(d * HA, HA)], a4r.at[d], twos[d])
+                az[4, d] = send(a_sum.at[pl.ds(A_FROM[d], A_HALF[d])], a4r.at[d, pl.ds(0, A_HALF[d])], twos[d])
                 continue
             at_row = (7 - 2 * step + d) * RA
             if step == 2:
                 az[4, d].wait_recv()
-                part = pl.ds(at_row + d * HA, HA)
-                a_sum[part, :] = a_sum[part, :] + a4r[d]
+                part = pl.ds(at_row + A_FROM[d], A_HALF[d])
+                a_sum[part, :] = a_sum[part, :] + a4r[d, : A_HALF[d], :]
                 az[3, d].wait_recv()
                 part = pl.ds(at_row, RA)
                 a_sum[part, :] = a_sum[part, :] + azr[2, d]
@@ -302,7 +306,8 @@
         lax.fori_loop(0, NX, one, 0)
         for h in range(NX):
             for d in range(2):
-                b4[h, d] = send(b4s.at[pl.ds(h * RB + d * HB, HB)], b4r.at[h, d], twos[d])
+                src = b4s.at[pl.ds(h * RB + B_FROM[d], B_HALF[d])]
+                b4[h, d] = send(src, b4r.at[h, d, pl.ds(0, B_HALF[d])], twos[d])
 
     def b_own(step, first, last):
         def one(n, _):
@@ -319,8 +324,8 @@
             src = bs.at[step - 1, h, d]
             if step == 2:
                 b4[h, d].wait_recv()
-                part = pl.ds(d * HB, HB)
-                src[part, :] = src[part, :] + b4r[h, d]
+                part = pl.ds(B_FROM[d], B_HALF[d])
+                src[part, :] = src[part, :] + b4r[h, d, : B_HALF[d], :]
             if step < 3:
                 bz[step + 1, h, d].wait_recv()
                 src[...] = src[...] + br[step, h, d]
@@ -366,23 +371,22 @@
             total = total + bxr[h]
         finish(RA, RB, total)
 
-    with jax.named_scope("reduce early"):
+    with jax.named_scope("reduce"):
         b_far()
         a_far(0)
-        b_own(3, 0, 2)
+        a_far(1)
+        b_own(3, 0, 4)
         b_z(3, 0)
         b_z(3, 1)
-        a_far(1)
-        b_own(3, 2, 4)
         b_z(3, 2)
         b_z(3, 3)
+        a_far(2)
         a_near(0, 3)
         b_own(2, 0, 4)
-    with jax.named_scope("reduce middle"):
         a_x(0)
-        a_x(1)
         b_z(2, 0)
         b_z(2, 1)
+        a_x(1)
         b_z(2, 2)
         b_z(2, 3)
         a_near(3, 8)
@@ -390,39 +394,42 @@
         a_x(3)
         a_x(4)
         b_own(1, 0, 4)
+        b_home()
         a_own()
-    with jax.named_scope("reduce late"):
         a_add(0)
         a_z(4)
         b_z(1, 0)
         b_z(1, 1)
+        b_z(1, 2)
+        b_z(1, 3)
         a_add(1)
         a_z(3)
-        b_z(1, 2)
-        b_z(1, 3)
-        b_home()
         a_add(2)
-        a_z(2)
         b_x(0)
         b_x(1)
+        b_x(2)
+        a_z(2)
         a_add(3)
         a_z(1)
-        b_x(2)
         b_x(3)
         a_add(4)
-    with jax.named_scope("reduce end"):
         b_finish()
         a_finish()
 
-    with jax.named_scope("spread over cols"):
-        for first in (RA, 0):
-            for o in range(1, NY):
-                spread[first, o].wait_recv()
+    def product(first, rows, before):
+        for o in range(1, NY):
+            spread[first, o].wait_recv()
+        part = pl.ds(first, rows)
+        mine_t = f_v[y, part, :].T
+        for c in range(NY):
+            whole = jnp.dot(mine_t, f_v[c, part, :], precision=lax.Precision.HIGHEST, preferred_element_type=F32)
+            lanes = slice(c * COLS, (c + 1) * COLS)
+            added = whole[:COLS, :COLS] + whole[COLS:, COLS:]
+            p_v[:, lanes] = p_v[:, lanes] + added if before else added
+
     with jax.named_scope("gram product"):
-        mine_t = f_v[y].T
-        for c in range(NY):
-            whole = jnp.dot(mine_t, f_v[c], precision=lax.Precision.HIGHEST, preferred_element_type=F32)
-            p_v[:, c * COLS : (c + 1) * COLS] = whole[:COLS, :COLS] + whole[COLS:, COLS:]
+        product(RA, RB, False)
+        product(0, RA, True)
 
     def corner_copy(src_of, dst, n):
         return [remote(src_of(to), dst, gs_sem.at[n], gr_sem.at[n], device) for to, device in corners]
@@ -487,7 +494,7 @@
         all_seven(g1r, n, gs_sem)
 
 
-MESSAGES = 4 + 10 + 8 + 8 + 24 + 3 + 8
+MESSAGES = 6 + 10 + 8 + 8 + 24 + 3 + 8
 
 
 def on_device(matrix_t, signs, sample_ids):
@@ -514,15 +521,15 @@
             vm((CHIPS, 1, LIST), I32),
             pltpu.SMEM((CHIPS, 1, LIST), I32),
             vm((LIST, 128), F32),
-            vm((2, NZ * HA, 128), F32),
-            vm((2, NZ * HA, 128), F32),
+            vm((2, NZ * A_HALF[0], 128), F32),
+            vm((2, NZ * A_HALF[0], 128), F32),
             vm((2, NZ * RA, 128), F32),
             vm((2, NZ * RA, 128), F32),
             vm((NZ * RA, 128), F32),
-            vm((2, HA, 128), F32),
+            vm((2, A_HALF[0], 128), F32),
             vm((3, 2, RA, 128), F32),
             vm((NX * RB, 128), F32),
-            vm((NX, 2, HB, 128), F32),
+            vm((NX, 2, B_HALF[0], 128), F32),
             vm((3, NX, 2, RB, 128), F32),
             vm((3, NX, 2, RB, 128), F32),
             vm((NX * RB, 128), F32),
@@ -545,6 +552,7 @@
             dma((MESSAGES,)),
             dma((3,)),
             dma((3,)),
+            pltpu.SemaphoreType.REGULAR,
         ],
         compiler_params=pltpu.CompilerParams(
             collective_id=0, has_side_effects=True, vmem_limit_bytes=40 << 20

time: 59.4 us -> 58.1 us (0.978)
  Pallas kernels: 58 us -> 56.7 us
    pallas_call x1, Pallas kernels: 58 us -> 56.7 us  [on_device(): pl.pallas_call(kernel, name='sketch_gram', out_shape=jax.ShapeDtypeStruct...]
where the time goes in v4:
time: 58.1 us; the launch traced here: 58 us
  Pallas kernels  56.7 us (98%)
  other arithmetic  0.66 us (1%)
  between operations  0.64 us (1%)
    pallas_call x1, Pallas kernels, on_device(): pl.pallas_call(kernel, name='sketch_gram', out_shape=jax.ShapeDtypeStruct...  56.7 us

profile of v4, /device:TPU:1, one launch (start us, length us, event | category | flops | bytes accessed | tf_op | source)
XLA Modules:
  0.0 58.0 jit_solution(1578076642777376209)
XLA Ops:
  0.6 56.7 %sketch_gram.1 = f32[128,256]{1,0:T(8,128)S(1)} custom-call(f32[64,8192]{1,0:T(8,128)} %m_ref.1, s32[64,128]{1,0:T(8,128)} %bitcast.2, s32[2,128]{1,0:T(2,128)} %bitcast.3), custom_call_target="tpu_custom_call" | custom-call | tf_op jit(solution)/shard_map/sketch_gram/pallas_call | solution.py:505
  57.4 0.7 %slice_multiply_fusion = (f32[64,256]{1,0:T(8,128)}, f32[64,256]{1,0:T(8,128)}) fusion(f32[128,256]{1,0:T(8,128)S(1)} %sketch_gram.1), kind=kLoop, calls=%fused_computation | loop fusion | flops 16384 | bytes 262144 | tf_op jit(solution)/shard_map/mul | solution.py:561

commit v5 on v4

--- a/solution.py
+++ b/solution.py
@@ -106,6 +106,10 @@
     for o in (2, -2):
         pl.semaphore_signal(far_sem, inc=1, device_id=at(x, z + o, core), device_id_type=MESH)
 
+    for to, device in corners:
+        remote(cls_v.at[lax.rem(to, 2)], idr_v.at[corner], is_sem.at[0], ir_sem.at[0], device).start()
+    idr_v[corner] = cls_v[core]
+
     sign_out = remote(s_ref, sp_v, ps_sem, pr_sem, partner)
     sign_out.start()
 
@@ -113,17 +117,16 @@
         piece = pl.ds(pl.multiple_of(q * 1024, 1024), 1024)
         return remote(m_ref.at[:, piece], xp_v.at[q], xs_sem.at[q], xr_sem.at[q], partner)
 
-    pair_copy(0).start()
+    for q in range(8):
+        pair_copy(q).start()
 
     def wait_all(ref, slots, sem):
         piece = ref.at[pl.ds(0, slots)]
         pltpu.make_async_copy(piece, piece, sem).wait()
 
-    for to, device in corners:
-        remote(cls_v.at[lax.rem(to, 2)], idr_v.at[corner], is_sem.at[0], ir_sem.at[0], device).start()
-    idr_v[corner] = cls_v[core]
-    for q in range(1, 8):
-        pair_copy(q).start()
+    def into_smem(level):
+        four = pl.ds(level * NX, NX)
+        return pltpu.make_async_copy(ids_v.at[four], ids_s.at[four], sm_sem.at[2])
 
     def lists_along_z():
         pl.semaphore_wait(far_sem, 2)
@@ -131,8 +134,9 @@
         for n in range(NX):
             ids_v[z * NX + n] = idr_v[2 * n] | ((idr_v[2 * n + 1] ^ (ROWS // 2)) << 16)
         four = ids_v.at[pl.ds(z * NX, NX)]
-        for device in heights:
-            remote(four, four, is_sem.at[1], ir_sem.at[1], device).start()
+        for o in (4, 3, 5, 2, 6, 1, 7):
+            remote(four, four, is_sem.at[1], ir_sem.at[o], heights[o - 1]).start()
+        into_smem(z).start()
 
     block = lax.broadcasted_iota(I32, (LIST, 128), 0) // KEEP
     parity = block & chip
@@ -184,10 +188,12 @@
             return 0
 
         lax.fori_loop(0, 16, across, 0)
-    wait_all(ids_v, 7 * NX, ir_sem.at[1])
-    lists = pltpu.make_async_copy(ids_v, ids_s, sm_sem.at[2])
-    lists.start()
-    lists.wait()
+    for o in (1, 7, 2, 6, 3, 5, 4):
+        level = lax.rem(z + NZ - o, NZ)
+        four = ids_v.at[pl.ds(level * NX, NX)]
+        remote(four, four, is_sem.at[1], ir_sem.at[o], heights[o - 1]).wait_recv()
+        into_smem(level).start()
+    pltpu.make_async_copy(ids_v, ids_s, sm_sem.at[2]).wait()
 
     half = lax.broadcasted_iota(I32, (1, 128), 1) < 64
 
@@ -547,7 +553,7 @@
             dma,
             dma,
             dma((2,)),
-            dma((2,)),
+            dma((8,)),
             dma((MESSAGES,)),
             dma((MESSAGES,)),
             dma((3,)),

time: 58.1 us -> 58 us (level)
  no operation moved by 1% of the time
where the time goes in v5:
time: 58 us; the launch traced here: 57.9 us
  Pallas kernels  56.6 us (98%)
  other arithmetic  0.66 us (1%)
  between operations  0.64 us (1%)
    pallas_call x1, Pallas kernels, on_device(): pl.pallas_call(kernel, name='sketch_gram', out_shape=jax.ShapeDtypeStruct...  56.6 us

profile of v5, /device:TPU:1, one launch (start us, length us, event | category | flops | bytes accessed | tf_op | source)
XLA Modules:
  0.0 57.9 jit_solution(16850621210370512183)
XLA Ops:
  0.6 56.6 %sketch_gram.1 = f32[128,256]{1,0:T(8,128)S(1)} custom-call(f32[64,8192]{1,0:T(8,128)} %m_ref.1, s32[64,128]{1,0:T(8,128)} %bitcast.2, s32[2,128]{1,0:T(2,128)} %bitcast.3), custom_call_target="tpu_custom_call" | custom-call | tf_op jit(solution)/shard_map/sketch_gram/pallas_call | solution.py:511
  57.2 0.7 %slice_multiply_fusion = (f32[64,256]{1,0:T(8,128)}, f32[64,256]{1,0:T(8,128)}) fusion(f32[128,256]{1,0:T(8,128)S(1)} %sketch_gram.1), kind=kLoop, calls=%fused_computation | loop fusion | flops 16384 | bytes 262144 | tf_op jit(solution)/shard_map/mul | solution.py:567
